TPU v7x, 512 devices: a whole 4x8x8 slice. The times are simulated.
512 devices in a mesh: row: 16 (over x_lo, z), col: 32 (over y, x_hi, core).
Axes of the slice: x: 4 (x_hi: 2, x_lo: 2; x = x_hi * 2 + x_lo), y: 8, z: 8, core: 2. Of those that a mesh axis runs over, the one named last changes fastest.
Arguments:
- projections: float32 [49152, 128], P(('row', 'col')), may hold values from -40 to 40
- partner: int32 [49152], P(('row', 'col')), may hold values from 0 to 49151, as said below
Outputs:
- losses: float32 [49152], P(('row', 'col'))
- grad: float32 [49152, 128], P(('row', 'col'))
Inputs may be any that keep to these rules, and one draw needn't show every extreme that they name: Each view's partner is another view of the same aligned block of 96 views, and the partner of a view's partner is the view itself.
All inputs are finite; a program needn't handle non-finite values.
Results may differ from a plain program's by a relative error of at most 0.0066.
Values may be sent and summed in bfloat16 or wider, within the bound.
A program may use at most 64 MiB of HBM per device.

v0:
```python
import math

import jax
import jax.numpy as jnp
from jax import lax
from jax.sharding import PartitionSpec as P

inv_temp = 10.0
epsilon = 1e-06


def block_count(total):
    return total // math.gcd(total, 512)


def exp_scores(block_unit, block_ids, col_unit, col_ids):
    scores = (
        jnp.einsum("rp,cp->rc", block_unit, col_unit, preferred_element_type=jnp.float32) * inv_temp
    )
    return jnp.where(block_ids[:, None] == col_ids[None, :], 0.0, jnp.exp(scores - inv_temp))


def row_totals(row_unit, row_ids, col_unit, col_ids):
    count = block_count(row_unit.shape[0])

    def block_sums(packed):
        return jnp.sum(exp_scores(packed[0], packed[1], col_unit, col_ids), axis=1)

    sums = lax.map(
        block_sums, (row_unit.reshape(count, -1, row_unit.shape[1]), row_ids.reshape(count, -1))
    )
    return sums.reshape(-1)


def weighted_terms(row_unit, row_ids, col_unit, col_ids, totals):
    count = block_count(row_unit.shape[0])
    width = row_unit.shape[1]

    def block_terms(carry, packed):
        block_unit, block_ids, block_totals = packed
        weights = (
            exp_scores(block_unit, block_ids, col_unit, col_ids) / block_totals[:, None]
        ).astype(jnp.bfloat16)
        row_out = jnp.dot(weights, col_unit, preferred_element_type=jnp.float32)
        carry = carry + jnp.einsum(
            "rc,rp->cp", weights, block_unit, preferred_element_type=jnp.float32
        )
        return (carry, row_out)

    start = jnp.zeros((col_unit.shape[0], width), jnp.float32)
    packed = (
        row_unit.reshape(count, -1, width),
        row_ids.reshape(count, -1),
        totals.reshape(count, -1),
    )
    col_out, row_out = lax.scan(block_terms, start, packed)
    return (row_out.reshape(-1, width), col_out)


def body(projections, partner):
    views = projections.shape[0]
    scale = lax.rsqrt(jnp.sum(projections * projections, axis=1, keepdims=True) + epsilon)
    unit = (projections * scale).astype(jnp.bfloat16)
    n_row = lax.axis_size("row")
    n_col = lax.axis_size("col")
    here_row = lax.axis_index("row")
    here_col = lax.axis_index("col")
    first = (here_row * n_col + here_col) * views
    local_partner = partner - first
    matches = (local_partner[:, None] == jnp.arange(views, dtype=jnp.int32)[None, :]).astype(
        jnp.bfloat16
    )
    partner_unit = jnp.dot(matches, unit, preferred_element_type=jnp.float32)
    positive = jnp.sum(unit.astype(jnp.float32) * partner_unit, axis=1) * inv_temp
    contiguous = jnp.arange(views * n_col, dtype=jnp.int32)
    strided = jnp.arange(views * n_row, dtype=jnp.int32)
    row_unit = lax.all_gather(unit, "col", axis=0, tiled=True)
    col_unit = lax.all_gather(unit, "row", axis=0, tiled=True)
    row_ids = here_row * n_col * views + contiguous
    col_ids = (strided // views * n_col + here_col) * views + strided % views
    partial_value = row_totals(row_unit, row_ids, col_unit, col_ids)
    totals = lax.psum(partial_value, "col")
    row_terms, col_terms = weighted_terms(row_unit, row_ids, col_unit, col_ids, totals)
    row_part = lax.psum_scatter(row_terms, "col", scatter_dimension=0, tiled=True)
    col_part = lax.psum_scatter(col_terms, "row", scatter_dimension=0, tiled=True)
    own_totals = lax.dynamic_slice_in_dim(totals, here_col * views, views)
    losses = inv_temp + jnp.log(own_totals) - positive
    dunit = inv_temp * (row_part + col_part - 2.0 * partner_unit)
    inner = jnp.sum(projections * dunit, axis=1, keepdims=True)
    grad = scale * dunit - scale * scale * scale * projections * inner
    return (losses, grad)


def solution(mesh):
    in_specs = (P(("row", "col"), None), P(("row", "col")))
    out_specs = (P(("row", "col")), P(("row", "col"), None))
    return jax.shard_map(body, mesh=mesh, in_specs=in_specs, out_specs=out_specs, check_vma=False)
```

profile of v0, /device:TPU:1, one launch (start us, length us, event | category | flops | bytes accessed | tf_op | source)
XLA Modules:
  0.0 454.5 jit_solution(4431187668975902097)
XLA Ops:
  9.6 45.8 %all_gather.6 = bf16[3072,128]{1,0:T(8,128)(2,1)S(1)} all-gather(bf16[96,128]{1,0:T(8,128)(2,1)S(1)} %multiply_convert_fusion), channel_id=1, replica_groups=mesh['row'=16,'col'=32] {'col'}, dimensions={0}, use_global_device_ids=true | all-gather | bytes 811008 | tf_op jit(solution)/shard_map/all_gather | solution.py:77
  55.4 33.5 %all_gather.7 = bf16[1536,128]{1,0:T(8,128)(2,1)S(1)} all-gather(bf16[96,128]{1,0:T(8,128)(2,1)S(1)} %multiply_convert_fusion), channel_id=1, replica_groups=mesh['row'=16,'col'=32] {'row'}, dimensions={0}, use_global_device_ids=true | all-gather | bytes 417792 | tf_op jit(solution)/shard_map/all_gather | solution.py:78
  88.9 6.5 %while.28 = (s32[]{:T(128)}, f32[6,512]{1,0:T(8,128)S(1)}, s32[6,512]{1,0:T(8,128)S(1)}, bf16[6,512,128]{2,1,0:T(8,128)(2,1)S(1)}, bf16[1536,128]{1,0:T(8,128)(2,1)S(1)}, /*index=5*/s32[]{:T(128)}, s32[]{:T(128)}, s32[]{:T(128)}) while((s32[]{:T(128)}, f32[6,512]{1,0:T(8,128)S(1)}, s32[6,512]{1,0:T(8,128)S(1)}, ...), condition=%wide.region_3.4_spmd.clone, body=%wide.region_1.3_spmd.clone.sunk | while | flops 205282816 | bytes 551013 | solution.py:29
  90.0 1.0 fusion.65
  92.2 1.0 fusion.65
  95.4 130.2 %psum.7 = f32[3072]{0:T(1024)S(1)} all-reduce(f32[3072]{0:T(1024)S(1)} %reshape.43), channel_id=1, replica_groups=mesh['row'=16,'col'=32] {'col'}, use_global_device_ids=true, to_apply=%region_4.5 | all-reduce | flops 3072 | bytes 24576 | tf_op jit(solution)/shard_map/psum | solution.py:82
  226.2 23.9 %while.29 = (s32[]{:T(128)}, f32[1536,128]{1,0:T(8,128)S(1)}, f32[6,512,128]{2,1,0:T(8,128)}, s32[6,512]{1,0:T(8,128)S(1)}, bf16[6,512,128]{2,1,0:T(8,128)(2,1)S...) while((s32[]{:T(128)}, f32[1536,128]{1,0:T(8,128)S(1)}, ...), condition=%wide.region_7.8_spmd.clone, body=%wide.region_6.7_spmd.clone.sunk | while | flops 609116160 | bytes 7629443 | solution.py:56
  226.9 1.0 divide_convert_fusion.2
  227.9 1.3 fusion.73
  230.9 1.0 divide_convert_fusion.2
  231.9 1.3 fusion.73
  234.9 1.0 divide_convert_fusion.2
  235.9 1.3 fusion.73
  238.9 1.0 divide_convert_fusion.2
  239.8 1.3 fusion.73
  242.8 1.0 divide_convert_fusion.2
  243.8 1.3 fusion.73
  246.8 1.0 divide_convert_fusion.2
  247.8 1.3 fusion.73
  251.8 59.4 %reduce-scatter.5.cloned.1.call-done = f32[96,128]{1,0:T(8,128)} async-done(((f32[1536,128]{1,0:T(8,128)}), f32[96,128]{1,0:T(8,128)}) %reduce-scatter.5.cloned.1.call-update) | async-done | bytes 49168 | tf_op jit(solution)/shard_map/reduce_scatter | solution.py:85
  311.1 132.6 %reduce-scatter.3.cloned.1.call-done = f32[96,128]{1,0:T(8,128)} async-done(((f32[3072,128]{1,0:T(8,128)}), f32[96,128]{1,0:T(8,128)}) %reduce-scatter.3.cloned.1.call-update) | async-done | bytes 49168 | tf_op jit(solution)/shard_map/reduce_scatter | solution.py:84
  443.7 1.1 multiply_reduce_fusion
  444.8 1.3 multiply_subtract_fusion.2
  446.2 1.5 multiply_subtract_fusion
  (76 shorter events, 19.1 us)
Async XLA Ops:
  7.2 304.0 %reduce-scatter.5.cloned.1.call-start = ((), (), s32[]{:S(2)}) async-start(), calls=%async_computation.3 | async-start | bytes 835584 | tf_op jit(solution)/shard_map/reduce_scatter | solution.py:85
  8.7 80.2 %copy-start.3 = (f32[96]{0:T(128)}, f32[96]{0:T(128)S(1)}, u32[]{:S(2)}) copy-start(f32[96]{0:T(128)S(1)} %get-tuple-element.261) | copy-start | bytes 1156
  225.6 0.6 copy-start.2
  250.1 0.9 copy-start
  250.1 1.7 copy-start.7
  250.1 193.6 %copy-start.1 = (f32[96,128]{1,0:T(8,128)S(1)}, f32[96,128]{1,0:T(8,128)}, u32[]{:S(2)}) copy-start(f32[96,128]{1,0:T(8,128)} %param.6) | copy-start | bytes 147460
  250.1 193.6 %copy-start.4 = (f32[96]{0:T(128)S(1)}, f32[96]{0:T(128)}, u32[]{:S(2)}) copy-start(f32[96]{0:T(128)} %copy-done.3) | copy-start | bytes 1156
  250.1 196.0 %copy-start.5 = (f32[96]{0:T(128)S(1)}, f32[96]{0:T(128)}, u32[]{:S(2)}) copy-start(f32[96]{0:T(128)} %get-tuple-element.259) | copy-start | bytes 1156
  250.1 196.0 %copy-start.6 = (f32[96]{0:T(128)S(1)}, f32[96]{0:T(128)}, u32[]{:S(2)}) copy-start(f32[96]{0:T(128)} %get-tuple-element.260) | copy-start | bytes 1156
  251.0 192.7 %reduce-scatter.3.cloned.1.call-start = ((), (), s32[]{:S(2)}) async-start(), calls=%async_computation.2 | async-start | bytes 1622016 | tf_op jit(solution)/shard_map/reduce_scatter | solution.py:84
Sparse Core Ops, SparseCore 0:
  251.1 59.9 reduce-scatter.4
  316.5 127.1 reduce-scatter.2
where the time goes:
time: 459 us; the launch traced here: 455 us
  blocking collectives  209 us (46%)
  waiting for transfers between devices  193 us (42%)
  matrix products  26.1 us (6%)
  between operations  14.2 us (3%)
  local copies, waits for them, and re-layouts  6.26 us (1%)
  other arithmetic  5.4 us (1%)
    reduce_scatter x1, waiting for transfers between devices, body(): lax.psum_scatter(row_terms, 'col', scatter_dimension=0, tiled=True)  133 us
    psum x1, blocking collectives, body(): totals = lax.psum(partial_value, 'col')  130 us
    reduce_scatter x1, waiting for transfers between devices, body(): lax.psum_scatter(col_terms, 'row', scatter_dimension=0, tiled=True)  59.4 us
    all_gather x1, blocking collectives, body(): row_unit = lax.all_gather(unit, 'col', axis=0, tiled=True)  45.8 us
    all_gather x1, blocking collectives, body(): col_unit = lax.all_gather(unit, 'row', axis=0, tiled=True)  33.5 us
    dot_general x12, matrix products, exp_scores(): jnp.einsum('rp,cp->rc', block_unit, col_unit, preferred_element_type=jnp....  11.6 us
  transfers between devices with their start and end apart: 2, of which 2 were waited for; matrix products, arithmetic and copies ran while one was open for 0% of the time, Pallas kernels for 0%

commit v1 on v0

v1 whole, which is shorter than its diff:
```python
import functools

import jax
import jax.numpy as jnp
from jax import lax
from jax.experimental import pallas as pl
from jax.experimental.pallas import tpu as pltpu
from jax.sharding import PartitionSpec as P

inv_temp = 10.0
epsilon = 1e-06
log2e = 1.4426950408889634

V = 96
W = 128
NX, NY, NZ, NC = 4, 8, 8, 2
NR = NX * NY * NC
GROUP = NX * V
BLOCK = NC * GROUP
COLS = NR * V
ROWS = NZ * V
TILE = 128
ORDER = (0, 1, 7, 2, 6, 3, 5, 4)
FAR = (4, 3, 5, 2, 6, 1, 7)

MESH = pl.DeviceIdType.MESH


def kernel(
    proj_hbm, partner_hbm, losses_ref, grad_ref,
    proj_ref, partner_ref, ur, cu, probs, acc, rhs, invc, tps, tp, tr, tc, sbuf, rbuf,
    in_sem, x_send, x_recv, y_send, y_recv, k_send, k_recv, z_send, z_recv,
    tp_send, tp_recv, tr_send, tr_recv, tc_send, tc_recv, o_send, o_recv,
):
    proj_copy = pltpu.make_async_copy(proj_hbm, proj_ref, in_sem.at[0])
    partner_copy = pltpu.make_async_copy(partner_hbm, partner_ref, in_sem.at[1])
    proj_copy.start()
    partner_copy.start()

    row, col = lax.axis_index("row"), lax.axis_index("col")
    z, x_lo = row % NZ, row // NZ
    core, x_hi, y = col % NC, (col // NC) % 2, col // (2 * NC)
    x = x_hi * 2 + x_lo
    at_x = [(x + dx) % NX for dx in range(NX)]
    x_row = [(px % 2) * NZ for px in at_x]
    x_col = [(px // 2) * NC for px in at_x]
    y_col = [((y + dy) % NY) * (2 * NC) for dy in range(NY)]
    at_z = [(z + dz) % NZ for dz in range(NZ)]
    cores = (core, 1 - core)

    def device(dx, dy, dz, dk):
        return (x_row[dx % NX] + at_z[dz % NZ], y_col[dy % NY] + x_col[dx % NX] + cores[dk])

    started = []

    def remote(src, dst, send_sem, recv_sem, to):
        return pltpu.make_async_remote_copy(
            src_ref=src, dst_ref=dst, send_sem=send_sem, recv_sem=recv_sem,
            device_id=to, device_id_type=MESH,
        )

    def send(*args):
        copy = remote(*args)
        copy.start()
        started.append(copy)
        return copy

    barrier = pltpu.get_barrier_semaphore()
    peers = [device(dx, 0, 0, 0) for dx in range(1, NX)]
    peers += [device(0, dy, 0, 0) for dy in range(1, NY)]
    peers += [device(0, 0, dz, 0) for dz in range(1, NZ)]
    peers += [device(0, 0, 0, 1)]
    for peer in peers:
        pl.semaphore_signal(barrier, inc=1, device_id=peer, device_id_type=MESH)

    tps[...] = jnp.ones_like(tps)
    proj_copy.wait()
    proj = proj_ref[...]
    scale = lax.rsqrt(jnp.sum(proj * proj, axis=1, keepdims=True) + epsilon)
    unit = (proj * scale).astype(jnp.bfloat16)
    ur[pl.ds(0, V), :] = unit
    cu[pl.ds(0, V), :] = unit

    pl.semaphore_wait(barrier, len(peers))

    def block(rank, dx):
        return ur.at[pl.ds(rank * BLOCK + dx * V, V)]

    def pass_on(rank, dx):
        return send(block(rank, 0), block(rank, dx), x_send.at[rank, dx], x_recv.at[rank, dx],
                    device(-dx, 0, 0, 0))

    for dx in (1, 3, 2):
        pass_on(0, dx)
    y_copies = [
        send(block(0, 0), block(rank, 0), y_send.at[rank], y_recv.at[rank],
             device(0, -ORDER[rank], 0, 0))
        for rank in range(1, NY)
    ]
    z_copies = [
        send(cu.at[pl.ds(0, V)], cu.at[pl.ds(dz * V, V)], z_send.at[dz], z_recv.at[dz],
             device(0, 0, -dz, 0))
        for dz in FAR
    ]
    for rank in range(1, NY):
        y_copies[rank - 1].wait_recv()
        for dx in (1, 3, 2):
            pass_on(rank, dx)

    def share(rank):
        first = rank * BLOCK
        return remote(ur.at[pl.ds(first, GROUP)], ur.at[pl.ds(first + GROUP, GROUP)],
                      k_send.at[rank], k_recv.at[rank], device(0, 0, 0, 1))

    def share_when_whole(rank):
        for dx in (1, 3, 2):
            remote(block(rank, 0), block(rank, dx), x_send.at[rank, dx], x_recv.at[rank, dx],
                   device(-dx, 0, 0, 0)).wait_recv()
        share(rank).start()

    def scores(rank, diagonal):
        first = pl.multiple_of(rank * BLOCK, BLOCK)
        units = ur[pl.ds(first, BLOCK), :]
        for at in range(0, ROWS, TILE):
            dots = lax.dot_general(
                cu[pl.ds(at, TILE), :], units, (((1,), (1,)), ((), ())),
                preferred_element_type=jnp.float32,
            )
            values = jnp.exp2(dots * (inv_temp * log2e))
            if diagonal and at == 0:
                views = lax.broadcasted_iota(jnp.int32, (TILE, BLOCK), 0)
                others = lax.broadcasted_iota(jnp.int32, (TILE, BLOCK), 1)
                values = jnp.where((views == others) & (views < V), 0.0, values)
            total = values[:, :W]
            for lane in range(W, BLOCK, W):
                total = total + values[:, lane:lane + W]
            if diagonal:
                acc[pl.ds(at, TILE), :] = total
            else:
                acc[pl.ds(at, TILE), :] += total
            probs[pl.ds(at, TILE), pl.ds(first, BLOCK)] = values.astype(jnp.bfloat16)

    share_when_whole(0)
    for copy in z_copies:
        copy.wait_recv()
    share_when_whole(1)
    share(0).wait_recv()
    scores(0, True)

    def step(rank, carry):
        @pl.when(rank < NY - 1)
        def _():
            share_when_whole(rank + 1)

        share(rank).wait_recv()
        scores(rank, False)
        return carry

    lax.fori_loop(1, NY, step, 0)

    ones = jnp.ones((8, W), jnp.float32)
    for dz in range(NZ):
        sums = lax.dot_general(
            ones, acc[pl.ds(dz * V, V), :], (((1,), (1,)), ((), ())),
            precision=lax.Precision.HIGHEST, preferred_element_type=jnp.float32,
        )
        tps[dz, :, pl.ds(0, V)] = sums[:1]
    tp[pl.ds(0, 1)] = tps[pl.ds(0, 1)]
    p_totals = [
        send(tps.at[pl.ds(dz, 1)], tp.at[pl.ds(dz, 1)], tp_send.at[dz], tp_recv.at[dz],
             device(0, 0, dz, 0))
        for dz in FAR
    ]

    partner_copy.wait()
    pairs = lax.broadcasted_iota(jnp.int32, (V, V), 0) + (row * (NY * 2 * NC) + col) * V
    pairs = (pairs == partner_ref[...]).astype(jnp.bfloat16)
    own_unit = ur[pl.ds(0, V), :]
    partner_unit = jnp.dot(pairs, own_unit, preferred_element_type=jnp.float32)
    positive = lax.dot_general(
        ones, own_unit.astype(jnp.float32) * partner_unit, (((1,), (1,)), ((), ())),
        precision=lax.Precision.HIGHEST, preferred_element_type=jnp.float32,
    )[:1] * inv_temp
    rhs[:, pl.ds(0, W)] = ur[...]

    for copy in p_totals:
        copy.wait_recv()
    totals = jnp.sum(tp[...], axis=0)
    tr[0] = totals
    tc[0] = totals
    for rank in range(NY - 1, -1, -1):
        for k in (1, 0):
            for dx in (2, 1, 3, 0):
                slot = (rank * NC + k) * NX + dx
                if slot:
                    remote(tr.at[pl.ds(0, 1)], tr.at[pl.ds(slot, 1)], tr_send, tr_recv,
                           device(-dx, -ORDER[rank], 0, k)).start()
    c_totals = [
        send(tc.at[pl.ds(0, 1)], tc.at[pl.ds(dz, 1)], tc_send.at[dz], tc_recv.at[dz],
             device(0, 0, -dz, 0))
        for dz in FAR
    ]
    losses_ref[...] = jnp.log(totals[:, :V]) - positive

    for copy in c_totals:
        copy.wait_recv()
    inverse = jnp.transpose(1.0 / tc[...].reshape(NZ, W))
    for dz in range(NZ):
        invc[pl.ds(dz * V, V), :] = jnp.broadcast_to(inverse[:V, dz:dz + 1], (V, W))

    rest = remote(tr.at[pl.ds(1, NR - 1)], tr.at[pl.ds(1, NR - 1)], tr_send, tr_recv, (row, col))
    rest.wait_recv()
    inverse = jnp.transpose(1.0 / tr[...].reshape(NR, W))
    for slot in range(NR):
        at = pl.ds(slot * V, V)
        rhs[at, pl.ds(W, W)] = (
            ur[at, :].astype(jnp.float32) * inverse[:V, slot:slot + 1]
        ).astype(jnp.bfloat16)

    outputs = []
    kept = None
    for dz in (4, 2, 6, 0):
        sums = jnp.dot(
            probs[pl.ds(dz * V, 2 * V), :], rhs[...], preferred_element_type=jnp.float32
        )
        part = sums[:, :W] * invc[pl.ds(dz * V, 2 * V), :] + sums[:, W:]
        if dz == 0:
            kept = part[:V]
            sbuf[pl.ds(V, V), :] = part[V:].astype(jnp.bfloat16)
        else:
            sbuf[pl.ds(dz * V, 2 * V), :] = part.astype(jnp.bfloat16)
        for to in (dz, dz + 1):
            if to:
                copy = send(sbuf.at[pl.ds(to * V, V)], rbuf.at[pl.ds(to * V, V)], o_send.at[to],
                            o_recv.at[to], device(0, 0, to, 0))
                outputs.append((to, copy))
    result = kept - 2.0 * partner_unit
    for to, copy in outputs:
        copy.wait_recv()
        result = result + rbuf[pl.ds(to * V, V), :].astype(jnp.float32)
    dunit = result * inv_temp
    proj = proj_ref[...]
    scale = lax.rsqrt(jnp.sum(proj * proj, axis=1, keepdims=True) + epsilon)
    inner = jnp.sum(proj * dunit, axis=1, keepdims=True)
    grad_ref[...] = scale * dunit - scale * scale * scale * proj * inner

    for copy in started:
        copy.wait_send()
    for rank in range(NY):
        share(rank).wait_send()
    rest.wait_send()


def body(projections, partner):
    dma = pltpu.SemaphoreType.DMA
    losses, grad = pl.pallas_call(
        kernel,
        out_shape=(
            jax.ShapeDtypeStruct((1, V), jnp.float32),
            jax.ShapeDtypeStruct((V, W), jnp.float32),
        ),
        in_specs=[pl.BlockSpec(memory_space=pl.ANY)] * 2,
        out_specs=(pl.BlockSpec(memory_space=pltpu.VMEM),) * 2,
        scratch_shapes=[
            pltpu.VMEM((V, W), jnp.float32),
            pltpu.VMEM((1, V), jnp.int32),
            pltpu.VMEM((COLS, W), jnp.bfloat16),
            pltpu.VMEM((ROWS, W), jnp.bfloat16),
            pltpu.VMEM((ROWS, COLS), jnp.bfloat16),
            pltpu.VMEM((ROWS, W), jnp.float32),
            pltpu.VMEM((COLS, 2 * W), jnp.bfloat16),
            pltpu.VMEM((ROWS, W), jnp.float32),
            pltpu.VMEM((NZ, 1, W), jnp.float32),
            pltpu.VMEM((NZ, 1, W), jnp.float32),
            pltpu.VMEM((NR, 1, W), jnp.float32),
            pltpu.VMEM((NZ, 1, W), jnp.float32),
            pltpu.VMEM((ROWS, W), jnp.bfloat16),
            pltpu.VMEM((ROWS, W), jnp.bfloat16),
            dma((2,)), dma((NY, NX)), dma((NY, NX)), dma((NY,)), dma((NY,)), dma((NY,)), dma((NY,)),
            dma((NZ,)), dma((NZ,)), dma((NZ,)), dma((NZ,)), dma, dma, dma((NZ,)), dma((NZ,)),
            dma((NZ,)), dma((NZ,)),
        ],
        compiler_params=pltpu.CompilerParams(
            collective_id=0, has_side_effects=True, vmem_limit_bytes=60 * 1024 * 1024
        ),
    )(projections, partner.reshape(1, V))
    return losses.reshape(V), grad


def solution(mesh):
    in_specs = (P(("row", "col"), None), P(("row", "col")))
    out_specs = (P(("row", "col")), P(("row", "col"), None))
    return jax.shard_map(body, mesh=mesh, in_specs=in_specs, out_specs=out_specs, check_vma=False)
```

time: 459 us -> 54.9 us (0.12)
  blocking collectives: 209 us -> 0 us
  waiting for transfers between devices: 193 us -> 0 us
  Pallas kernels: 0 us -> 51.5 us
  matrix products: 26.1 us -> 0 us
  between operations: 14.2 us -> 0.65 us
  other arithmetic: 5.4 us -> 0 us
    reduce_scatter x2 -> x0, waiting for transfers between devices: 192 us -> none  [the longest x1 133 us: body(): lax.psum_scatter(row_terms, 'col', scatter_dimension=0, tiled=True)]
    psum x1 -> x0, blocking collectives: 130 us -> none  [body(): totals = lax.psum(partial_value, 'col')]
    all_gather x2 -> x0, blocking collectives: 79.3 us -> none  [the longest x1 45.8 us: body(): row_unit = lax.all_gather(unit, 'col', axis=0, tiled=True)]
    pallas_call x0 -> x1, Pallas kernels: none -> 51.5 us  [body(): pl.pallas_call(kernel, out_shape=(jax.ShapeDtypeStruct((1, V), jnp.float3...]
    dot_general x25 -> x0, matrix products: 26.1 us -> none  [the longest x12 11.6 us: exp_scores(): jnp.einsum('rp,cp->rc', block_unit, col_unit, preferred_element_type=jnp....]
  transfers between devices with their start and end apart: 2 -> 0, of which waited for: 2 -> 0; matrix products, arithmetic and copies ran while one was open for 0% -> 0% of each run, Pallas kernels for 0% -> 0%
where the time goes in v1:
time: 54.9 us; the launch traced here: 54.6 us
  Pallas kernels  51.5 us (94%)
  local copies, waits for them, and re-layouts  2.53 us (5%)
  between operations  0.65 us (1%)
    pallas_call x1, Pallas kernels, body(): pl.pallas_call(kernel, out_shape=(jax.ShapeDtypeStruct((1, V), jnp.float3...  51.5 us
    unnamed x4, local copies, waits for them, and re-layouts  2.53 us

profile of v1, /device:TPU:1, one launch (start us, length us, event | category | flops | bytes accessed | tf_op | source)
XLA Modules:
  0.0 54.6 jit_solution(7967567136431543627)
XLA Ops:
  0.6 51.5 %shard_map.41 = (f32[1,96]{1,0:T(1,128)}, f32[96,128]{1,0:T(8,128)}) custom-call(f32[96,128]{1,0:T(8,128)} %proj_hbm.1, s32[1,96]{1,0:T(1,128)} %bitcast.2), custom_call_target="tpu_custom_call" | custom-call | tf_op jit(solution)/shard_map/pallas_call | solution.py:256
  52.1 0.0 copy-start
  52.1 0.6 %copy-done = f32[1,96]{1,0:T(1,128)S(1)} copy-done((f32[1,96]{1,0:T(1,128)S(1)}, f32[1,96]{1,0:T(1,128)}, u32[]{:S(2)}) %copy-start) | copy-done | bytes 408
  52.7 0.5 copy.6
  53.2 1.4 %copy.7 = f32[96,128]{1,0:T(8,128)} copy(f32[96,128]{1,0:T(8,128)} %get-tuple-element.9) | data formatting | bytes 98304
Async XLA Ops:
  52.1 0.6 %copy-start = (f32[1,96]{1,0:T(1,128)S(1)}, f32[1,96]{1,0:T(1,128)}, u32[]{:S(2)}) copy-start(f32[1,96]{1,0:T(1,128)} %get-tuple-element.4) | copy-start | bytes 1156

commit v2 on v1

v2 whole, which is shorter than its diff:
```python
import functools

import jax
import jax.numpy as jnp
from jax import lax
from jax.experimental import pallas as pl
from jax.experimental.pallas import tpu as pltpu
from jax.sharding import PartitionSpec as P

inv_temp = 10.0
epsilon = 1e-06
log2e = 1.4426950408889634

V = 96
W = 128
NX, NY, NZ, NC = 4, 8, 8, 2
NR = NX * NY * NC
GROUP = NX * V
BLOCK = NC * GROUP
COLS = NR * V
ROWS = NZ * V
TILE = 256
ORDER = (0, 1, 7, 2, 6, 3, 5, 4)

MESH = pl.DeviceIdType.MESH


def to_rows(tiles):
    rows = []
    for at in range(0, len(tiles), 3):
        first, second, third = tiles[at:at + 3]
        lane = lax.broadcasted_iota(jnp.int32, first.shape, first.ndim - 1)
        turn = functools.partial(pltpu.roll, axis=first.ndim - 1)
        rows.append(first)
        rows.append(jnp.where(lane < 32, turn(first, 32), turn(second, 32)))
        rows.append(jnp.where(lane < 64, turn(second, 64), turn(third, 64)))
        rows.append(turn(third, 96))
    return rows


def to_lanes(rows):
    tiles = []
    for at in range(0, len(rows), 4):
        first, second, third, fourth = rows[at:at + 4]
        lane = lax.broadcasted_iota(jnp.int32, first.shape, first.ndim - 1)
        turn = functools.partial(pltpu.roll, axis=first.ndim - 1)
        second, third, fourth = turn(second, 96), turn(third, 64), turn(fourth, 32)
        tiles.append(jnp.where(lane < 96, first, second))
        tiles.append(jnp.where(lane < 64, second, third))
        tiles.append(jnp.where(lane < 32, third, fourth))
    return tiles


def kernel(
    proj_hbm, partner_hbm, losses_ref, grad_ref,
    proj_ref, partner_ref, ur, cu, probs, acc, ut, uts, plain, tps, tp, to, tr, sbuf, rbuf,
    in_sem, x_send, x_recv, y_send, y_recv, k_send, k_recv, z_send, z_recv,
    tp_send, tp_recv, tr_send, tr_recv, tc_send, tc_recv, o_send, o_recv,
):
    proj_copy = pltpu.make_async_copy(proj_hbm, proj_ref, in_sem.at[0])
    partner_copy = pltpu.make_async_copy(partner_hbm, partner_ref, in_sem.at[1])
    proj_copy.start()
    partner_copy.start()

    row, col = lax.axis_index("row"), lax.axis_index("col")
    z, x_lo = row % NZ, row // NZ
    core, x_hi, y = col % NC, (col // NC) % 2, col // (2 * NC)
    x = x_hi * 2 + x_lo
    at_x = [(x + dx) % NX for dx in range(NX)]
    x_row = [(px % 2) * NZ for px in at_x]
    x_col = [(px // 2) * NC for px in at_x]
    y_col = [((y + dy) % NY) * (2 * NC) for dy in range(NY)]
    at_z = [(z + dz) % NZ for dz in range(NZ)]
    cores = (core, 1 - core)

    def device(dx, dy, dz, dk):
        return (x_row[dx % NX] + at_z[dz % NZ], y_col[dy % NY] + x_col[dx % NX] + cores[dk])

    started = []

    def remote(src, dst, send_sem, recv_sem, to):
        return pltpu.make_async_remote_copy(
            src_ref=src, dst_ref=dst, send_sem=send_sem, recv_sem=recv_sem,
            device_id=to, device_id_type=MESH,
        )

    def send(*args):
        copy = remote(*args)
        copy.start()
        started.append(copy)
        return copy

    barrier = pltpu.get_barrier_semaphore()
    peers = [device(dx, 0, 0, 0) for dx in range(1, NX)]
    peers += [device(0, dy, 0, 0) for dy in range(1, NY)]
    peers += [device(0, 0, dz, 0) for dz in range(1, NZ)]
    peers += [device(0, 0, dz, 1) for dz in range(NZ)]
    for peer in peers:
        pl.semaphore_signal(barrier, inc=1, device_id=peer, device_id_type=MESH)

    tps[...] = jnp.ones_like(tps)
    proj_copy.wait()
    proj = proj_ref[...]
    scale = lax.rsqrt(jnp.sum(proj * proj, axis=1, keepdims=True) + epsilon)
    unit = (proj * scale).astype(jnp.bfloat16)
    ur[pl.ds(0, V), :] = unit
    cu[pl.ds(0, V), :] = unit

    pl.semaphore_wait(barrier, len(peers))

    def block(rank, dx):
        return ur.at[pl.ds(rank * BLOCK + dx * V, V)]

    def to_x(rank, dx):
        return remote(block(rank, 0), block(rank, dx), x_send.at[rank, dx], x_recv.at[rank, dx],
                      device(-dx, 0, 0, 0))

    def pass_on(rank):
        for dx in (1, 3, 2):
            to_x(rank, dx).start()

    def share(rank):
        first = rank * BLOCK
        return remote(ur.at[pl.ds(first, GROUP)], ur.at[pl.ds(first + GROUP, GROUP)],
                      k_send.at[rank], k_recv.at[rank], device(0, 0, 0, 1))

    def share_when_whole(rank):
        for dx in (1, 3, 2):
            to_x(rank, dx).wait_recv()
        share(rank).start()

    def scores(rank, k, diagonal=False):
        first = pl.multiple_of((rank * NC + k) * GROUP, GROUP)
        rows = pl.ds(first, GROUP)
        units = ur[rows, :]
        ut[:, rows] = jnp.transpose(units)
        for lane in range(0, ROWS, TILE):
            lanes = pl.ds(lane, TILE)
            dots = lax.dot_general(
                units, cu[lanes, :], (((1,), (1,)), ((), ())), preferred_element_type=jnp.float32
            )
            values = jnp.exp2(dots * (inv_temp * log2e))
            if diagonal and lane == 0:
                left = lax.broadcasted_iota(jnp.int32, (GROUP, TILE), 0)
                right = lax.broadcasted_iota(jnp.int32, (GROUP, TILE), 1)
                values = jnp.where((left == right) & (left < V), 0.0, values)
            total = jnp.sum(values.reshape(GROUP // 8, 8, TILE), axis=0)
            probs[rows, lanes] = values.astype(jnp.bfloat16)
            if diagonal:
                acc[:, lanes] = total
            else:
                acc[:, lanes] += total

    pass_on(0)
    y_copies, z_copies = [], []
    for rank in range(1, NY):
        y_copies.append(send(block(0, 0), block(rank, 0), y_send.at[rank], y_recv.at[rank],
                             device(0, -ORDER[rank], 0, 0)))
        z_copies.append(send(cu.at[pl.ds(0, V)], cu.at[pl.ds(rank * V, V)], z_send.at[rank],
                             z_recv.at[rank], device(0, 0, -ORDER[rank], 0)))

    def arrived(copies, *ranks):
        for rank in ranks:
            copies[rank - 1].wait_recv()

    for rank in range(1, NY):
        arrived(y_copies, rank)
        pass_on(rank)
    share_when_whole(0)
    arrived(z_copies, *range(1, NZ))
    scores(0, 0, True)

    def own_core(rank, carry):
        share_when_whole(rank)
        scores(rank, 0)
        return carry

    def other_core(rank, carry):
        share(rank).wait_recv()
        scores(rank, 1)
        return carry

    lax.fori_loop(1, NY, own_core, 0)
    lax.fori_loop(0, NY, other_core, 0)

    sums = jnp.sum(acc[...], axis=0, keepdims=True)
    for rank, part in enumerate(to_rows([sums[:, at:at + W] for at in range(0, ROWS, W)])):
        tps[rank] = part
    p_totals = []
    for rank in range(NZ - 1, -1, -1):
        if rank:
            p_totals.append(send(tps, tp.at[rank], tp_send.at[rank], tp_recv.at[rank],
                                 device(0, 0, ORDER[rank], 0)))
        p_totals.append(send(tps.at[pl.ds(rank, 1)], to.at[pl.ds(rank, 1)], tc_send.at[rank],
                             tc_recv.at[rank], device(0, 0, ORDER[rank], 1)))

    partner_copy.wait()
    pairs = lax.broadcasted_iota(jnp.int32, (V, V), 0) + (row * (NY * 2 * NC) + col) * V
    pairs = (pairs == partner_ref[...]).astype(jnp.bfloat16)
    own_unit = ur[pl.ds(0, V), :]
    partner_unit = jnp.dot(pairs, own_unit, preferred_element_type=jnp.float32)
    positive = lax.dot_general(
        jnp.ones((8, W), jnp.float32), own_unit.astype(jnp.float32) * partner_unit, (((1,), (1,)), ((), ())),
        precision=lax.Precision.HIGHEST, preferred_element_type=jnp.float32,
    )[:1] * inv_temp

    def plain_sums(*lanes):
        for lane in lanes:
            plain[:, pl.ds(lane, TILE)] = jnp.dot(
                ut[...], probs[:, pl.ds(lane, TILE)], preferred_element_type=jnp.float32
            )

    plain_sums(0, TILE)
    for copy in p_totals:
        copy.wait_recv()
    where = {offset: rank for rank, offset in enumerate(ORDER)}
    totals_of = []
    for rank in range(NZ):
        total = tps[rank]
        for sender in range(1, NZ):
            total = total + tp[sender, where[(ORDER[rank] + ORDER[sender]) % NZ]]
        totals_of.append(total)
    totals = totals_of[0]
    tr[0] = jnp.concatenate([totals, jnp.sum(to[...], axis=0)], axis=0)
    for rank in range(NY - 1, -1, -1):
        for dx in (2, 1, 3, 0):
            if rank or dx:
                remote(tr.at[pl.ds(0, 1)], tr.at[pl.ds(rank * NX + dx, 1)], tr_send, tr_recv,
                       device(-dx, -ORDER[rank], 0, 0)).start()
    losses_ref[...] = jnp.log(totals[:, :V]) - positive
    inverse = [1.0 / part for part in to_lanes(totals_of)]
    plain_sums(2 * TILE)

    rest = remote(tr.at[pl.ds(1, NX * NY - 1)], tr.at[pl.ds(1, NX * NY - 1)], tr_send, tr_recv,
                  (row, col))
    rest.wait_recv()
    shares_of = tr[...].reshape(NY, NX, NC, W)
    scales = [1.0 / part for part in to_lanes([shares_of[:, dx] for dx in range(NX)])]
    for at in range(0, COLS, W):
        group, tile = at // GROUP, at % GROUP // W
        factor = scales[tile][group // NC, group % NC:group % NC + 1]
        uts[:, pl.ds(at, W)] = (ut[:, pl.ds(at, W)].astype(jnp.float32) * factor).astype(
            jnp.bfloat16
        )

    outputs = []
    for lane in range(ROWS - TILE, -1, -TILE):
        lanes = pl.ds(lane, TILE)
        sums = jnp.dot(uts[...], probs[:, lanes], preferred_element_type=jnp.float32)
        factor = jnp.concatenate(inverse[lane // W:(lane + TILE) // W], axis=1)
        part = jnp.transpose(plain[:, lanes] * factor + sums)
        sbuf[lanes, :] = part.astype(jnp.bfloat16)
        for rank in range(NZ - 1, 0, -1):
            if lane <= rank * V < lane + TILE:
                at = pl.ds(rank * V, V)
                copy = send(sbuf.at[at], rbuf.at[at], o_send.at[rank], o_recv.at[rank],
                            device(0, 0, ORDER[rank], 0))
                outputs.append((rank, copy))
    kept = part[:V]
    result = kept - 2.0 * partner_unit
    for rank, copy in outputs:
        copy.wait_recv()
        result = result + rbuf[pl.ds(rank * V, V), :].astype(jnp.float32)
    dunit = result * inv_temp
    proj = proj_ref[...]
    scale = lax.rsqrt(jnp.sum(proj * proj, axis=1, keepdims=True) + epsilon)
    inner = jnp.sum(proj * dunit, axis=1, keepdims=True)
    grad_ref[...] = scale * dunit - scale * scale * scale * proj * inner

    for copy in started:
        copy.wait_send()
    for rank in range(NY):
        for dx in (1, 3, 2):
            to_x(rank, dx).wait_send()
        share(rank).wait_send()
    rest.wait_send()


def body(projections, partner):
    dma = pltpu.SemaphoreType.DMA
    projections = pltpu.with_memory_space_constraint(projections, pltpu.HBM)
    partner = pltpu.with_memory_space_constraint(partner.reshape(1, V), pltpu.HBM)
    losses, grad = pl.pallas_call(
        kernel,
        out_shape=(pltpu.VMEM((1, V), jnp.float32), pltpu.VMEM((V, W), jnp.float32)),
        in_specs=[pl.BlockSpec(memory_space=pl.ANY)] * 2,
        out_specs=(pl.BlockSpec(memory_space=pltpu.VMEM),) * 2,
        scratch_shapes=[
            pltpu.VMEM((V, W), jnp.float32),
            pltpu.VMEM((1, V), jnp.int32),
            pltpu.VMEM((COLS, W), jnp.bfloat16),
            pltpu.VMEM((ROWS, W), jnp.bfloat16),
            pltpu.VMEM((COLS, ROWS), jnp.bfloat16),
            pltpu.VMEM((8, ROWS), jnp.float32),
            pltpu.VMEM((W, COLS), jnp.bfloat16),
            pltpu.VMEM((W, COLS), jnp.bfloat16),
            pltpu.VMEM((W, ROWS), jnp.float32),
            pltpu.VMEM((NZ, 1, W), jnp.float32),
            pltpu.VMEM((NZ, NZ, 1, W), jnp.float32),
            pltpu.VMEM((NZ, 1, W), jnp.float32),
            pltpu.VMEM((NY * NX, NC, W), jnp.float32),
            pltpu.VMEM((ROWS, W), jnp.bfloat16),
            pltpu.VMEM((ROWS, W), jnp.bfloat16),
            dma((2,)), dma((NY, NX)), dma((NY, NX)), dma((NY,)), dma((NY,)), dma((NY,)), dma((NY,)),
            dma((NZ,)), dma((NZ,)), dma((NZ,)), dma((NZ,)), dma, dma, dma((NZ,)), dma((NZ,)),
            dma((NZ,)), dma((NZ,)),
        ],
        compiler_params=pltpu.CompilerParams(
            collective_id=0, has_side_effects=True, vmem_limit_bytes=48 * 1024 * 1024
        ),
    )(projections, partner)
    return losses.reshape(V), grad


def solution(mesh):
    in_specs = (P(("row", "col"), None), P(("row", "col")))
    out_specs = (P(("row", "col")), P(("row", "col"), None))
    return jax.shard_map(body, mesh=mesh, in_specs=in_specs, out_specs=out_specs, check_vma=False)
```

time: 54.9 us -> 52.3 us (0.953)
  local copies, waits for them, and re-layouts: 2.53 us -> 1.13 us
  Pallas kernels: 51.5 us -> 50.4 us
    unnamed x4 -> x2, local copies, waits for them, and re-layouts: 2.53 us -> 1.13 us
    pallas_call x1, Pallas kernels: 51.5 us -> 50.4 us  [body(): pl.pallas_call(kernel, out_shape=(pltpu.VMEM((1, V), jnp.float32), pltpu....]
where the time goes in v2:
time: 52.3 us; the launch traced here: 52.2 us
  Pallas kernels  50.4 us (96%)
  local copies, waits for them, and re-layouts  1.13 us (2%)
  between operations  0.64 us (1%)
    pallas_call x1, Pallas kernels, body(): pl.pallas_call(kernel, out_shape=(pltpu.VMEM((1, V), jnp.float32), pltpu....  50.4 us
    unnamed x2, local copies, waits for them, and re-layouts  1.13 us

profile of v2, /device:TPU:1, one launch (start us, length us, event | category | flops | bytes accessed | tf_op | source)
XLA Modules:
  0.0 52.2 jit_solution(12118408256144604503)
XLA Ops:
  0.6 50.4 %shard_map.41 = (f32[1,96]{1,0:T(1,128)S(1)}, f32[96,128]{1,0:T(8,128)S(1)}) custom-call(f32[96,128]{1,0:T(8,128)} %proj_hbm.1, s32[1,96]{1,0:T(1,128)} %bitcast.3), custom_call_target="tpu_custom_call" | custom-call | tf_op jit(solution)/shard_map/pallas_call | solution.py:283
  51.0 0.5 copy.6
  51.5 0.6 %copy.7 = f32[96,128]{1,0:T(8,128)} copy(f32[96,128]{1,0:T(8,128)S(1)} %get-tuple-element.7) | data formatting | bytes 98304

commit v3 on v2

--- a/solution.py
+++ b/solution.py
@@ -12,6 +12,7 @@
 log2e = 1.4426950408889634
 
 V = 96
+HALF = V // 2
 W = 128
 NX, NY, NZ, NC = 4, 8, 8, 2
 NR = NX * NY * NC
@@ -53,8 +54,8 @@
 
 def kernel(
     proj_hbm, partner_hbm, losses_ref, grad_ref,
-    proj_ref, partner_ref, ur, cu, probs, acc, ut, uts, plain, tps, tp, to, tr, sbuf, rbuf,
-    in_sem, x_send, x_recv, y_send, y_recv, k_send, k_recv, z_send, z_recv,
+    proj_ref, partner_ref, ur, cu, probs, acc, both, tps, tp, to, tr, sbuf, rbuf,
+    in_sem, x_send, x_recv, y_send, y_recv, f_send, f_recv, k_send, k_recv, z_send, z_recv,
     tp_send, tp_recv, tr_send, tr_recv, tc_send, tc_recv, o_send, o_recv,
 ):
     proj_copy = pltpu.make_async_copy(proj_hbm, proj_ref, in_sem.at[0])
@@ -108,12 +109,19 @@
 
     pl.semaphore_wait(barrier, len(peers))
 
-    def block(rank, dx):
-        return ur.at[pl.ds(rank * BLOCK + dx * V, V)]
+    def block(rank, dx, half=None):
+        first = rank * BLOCK + dx * V
+        return ur.at[pl.ds(first, V)] if half is None else ur.at[pl.ds(first + half * HALF, HALF)]
 
     def to_x(rank, dx):
-        return remote(block(rank, 0), block(rank, dx), x_send.at[rank, dx], x_recv.at[rank, dx],
-                      device(-dx, 0, 0, 0))
+        half = 1 if dx == 2 and not (isinstance(rank, int) and rank == 0) else None
+        return remote(block(rank, 0, half), block(rank, dx, half), x_send.at[rank, dx],
+                      x_recv.at[rank, dx], device(-dx, 0, 0, 0))
+
+    def from_far(rank):
+        dy = ORDER[rank] if isinstance(rank, int) else 1
+        return remote(block(0, 2, 0), block(rank, 2, 0), f_send.at[rank], f_recv.at[rank],
+                      device(0, -dy, 0, 0))
 
     def pass_on(rank):
         for dx in (1, 3, 2):
@@ -125,15 +133,17 @@
                       k_send.at[rank], k_recv.at[rank], device(0, 0, 0, 1))
 
     def share_when_whole(rank):
-        for dx in (1, 3, 2):
+        for dx in (1, 3) if isinstance(rank, int) and rank == 0 else (1, 3, 2):
             to_x(rank, dx).wait_recv()
+        if not (isinstance(rank, int) and rank == 0):
+            from_far(rank).wait_recv()
         share(rank).start()
 
     def scores(rank, k, diagonal=False):
         first = pl.multiple_of((rank * NC + k) * GROUP, GROUP)
         rows = pl.ds(first, GROUP)
         units = ur[rows, :]
-        ut[:, rows] = jnp.transpose(units)
+        both[pl.ds(0, W), rows] = jnp.transpose(units)
         for lane in range(0, ROWS, TILE):
             lanes = pl.ds(lane, TILE)
             dots = lax.dot_general(
@@ -163,7 +173,14 @@
         for rank in ranks:
             copies[rank - 1].wait_recv()
 
+    arrived(y_copies, 1)
+    pass_on(1)
+    arrived(y_copies, 2)
+    pass_on(2)
+    to_x(0, 2).wait_recv()
     for rank in range(1, NY):
+        from_far(rank).start()
+    for rank in range(3, NY):
         arrived(y_copies, rank)
         pass_on(rank)
     share_when_whole(0)
@@ -180,8 +197,14 @@
         scores(rank, 1)
         return carry
 
-    lax.fori_loop(1, NY, own_core, 0)
-    lax.fori_loop(0, NY, other_core, 0)
+    def both_cores(rank, carry):
+        own_core(rank, carry)
+        other_core(rank - 2, carry)
+        return carry
+
+    own_core(1, 0)
+    lax.fori_loop(2, NY, both_cores, 0)
+    lax.fori_loop(NY - 2, NY, other_core, 0)
 
     sums = jnp.sum(acc[...], axis=0, keepdims=True)
     for rank, part in enumerate(to_rows([sums[:, at:at + W] for at in range(0, ROWS, W)])):
@@ -204,13 +227,6 @@
         precision=lax.Precision.HIGHEST, preferred_element_type=jnp.float32,
     )[:1] * inv_temp
 
-    def plain_sums(*lanes):
-        for lane in lanes:
-            plain[:, pl.ds(lane, TILE)] = jnp.dot(
-                ut[...], probs[:, pl.ds(lane, TILE)], preferred_element_type=jnp.float32
-            )
-
-    plain_sums(0, TILE)
     for copy in p_totals:
         copy.wait_recv()
     where = {offset: rank for rank, offset in enumerate(ORDER)}
@@ -229,7 +245,6 @@
                        device(-dx, -ORDER[rank], 0, 0)).start()
     losses_ref[...] = jnp.log(totals[:, :V]) - positive
     inverse = [1.0 / part for part in to_lanes(totals_of)]
-    plain_sums(2 * TILE)
 
     rest = remote(tr.at[pl.ds(1, NX * NY - 1)], tr.at[pl.ds(1, NX * NY - 1)], tr_send, tr_recv,
                   (row, col))
@@ -239,16 +254,16 @@
     for at in range(0, COLS, W):
         group, tile = at // GROUP, at % GROUP // W
         factor = scales[tile][group // NC, group % NC:group % NC + 1]
-        uts[:, pl.ds(at, W)] = (ut[:, pl.ds(at, W)].astype(jnp.float32) * factor).astype(
-            jnp.bfloat16
-        )
+        both[pl.ds(W, W), pl.ds(at, W)] = (
+            both[pl.ds(0, W), pl.ds(at, W)].astype(jnp.float32) * factor
+        ).astype(jnp.bfloat16)
 
     outputs = []
     for lane in range(ROWS - TILE, -1, -TILE):
         lanes = pl.ds(lane, TILE)
-        sums = jnp.dot(uts[...], probs[:, lanes], preferred_element_type=jnp.float32)
+        sums = jnp.dot(both[...], probs[:, lanes], preferred_element_type=jnp.float32)
         factor = jnp.concatenate(inverse[lane // W:(lane + TILE) // W], axis=1)
-        part = jnp.transpose(plain[:, lanes] * factor + sums)
+        part = jnp.transpose(sums[:W] * factor + sums[W:])
         sbuf[lanes, :] = part.astype(jnp.bfloat16)
         for rank in range(NZ - 1, 0, -1):
             if lane <= rank * V < lane + TILE:
@@ -272,6 +287,8 @@
     for rank in range(NY):
         for dx in (1, 3, 2):
             to_x(rank, dx).wait_send()
+        if rank:
+            from_far(rank).wait_send()
         share(rank).wait_send()
     rest.wait_send()
 
@@ -292,9 +309,7 @@
             pltpu.VMEM((ROWS, W), jnp.bfloat16),
             pltpu.VMEM((COLS, ROWS), jnp.bfloat16),
             pltpu.VMEM((8, ROWS), jnp.float32),
-            pltpu.VMEM((W, COLS), jnp.bfloat16),
-            pltpu.VMEM((W, COLS), jnp.bfloat16),
-            pltpu.VMEM((W, ROWS), jnp.float32),
+            pltpu.VMEM((2 * W, COLS), jnp.bfloat16),
             pltpu.VMEM((NZ, 1, W), jnp.float32),
             pltpu.VMEM((NZ, NZ, 1, W), jnp.float32),
             pltpu.VMEM((NZ, 1, W), jnp.float32),
@@ -302,6 +317,7 @@
             pltpu.VMEM((ROWS, W), jnp.bfloat16),
             pltpu.VMEM((ROWS, W), jnp.bfloat16),
             dma((2,)), dma((NY, NX)), dma((NY, NX)), dma((NY,)), dma((NY,)), dma((NY,)), dma((NY,)),
+            dma((NY,)), dma((NY,)),
             dma((NZ,)), dma((NZ,)), dma((NZ,)), dma((NZ,)), dma, dma, dma((NZ,)), dma((NZ,)),
             dma((NZ,)), dma((NZ,)),
         ],

time: 52.3 us -> 51.8 us (level)
  no operation moved by 1% of the time
where the time goes in v3:
time: 51.8 us; the launch traced here: 51.6 us
  Pallas kernels  49.9 us (96%)
  local copies, waits for them, and re-layouts  1.13 us (2%)
  between operations  0.64 us (1%)
    pallas_call x1, Pallas kernels, body(): pl.pallas_call(kernel, out_shape=(pltpu.VMEM((1, V), jnp.float32), pltpu....  49.9 us
    unnamed x2, local copies, waits for them, and re-layouts  1.13 us

profile of v3, /device:TPU:1, one launch (start us, length us, event | category | flops | bytes accessed | tf_op | source)
XLA Modules:
  0.0 51.6 jit_solution(8828093562979602866)
XLA Ops:
  0.6 49.9 %shard_map.41 = (f32[1,96]{1,0:T(1,128)S(1)}, f32[96,128]{1,0:T(8,128)S(1)}) custom-call(f32[96,128]{1,0:T(8,128)} %proj_hbm.1, s32[1,96]{1,0:T(1,128)} %bitcast.3), custom_call_target="tpu_custom_call" | custom-call | tf_op jit(solution)/shard_map/pallas_call | solution.py:300
  50.5 0.5 copy.6
  51.0 0.6 %copy.7 = f32[96,128]{1,0:T(8,128)} copy(f32[96,128]{1,0:T(8,128)S(1)} %get-tuple-element.7) | data formatting | bytes 98304

commit v4 on v2

--- a/solution.py
+++ b/solution.py
@@ -14,11 +14,10 @@
 V = 96
 W = 128
 NX, NY, NZ, NC = 4, 8, 8, 2
-NR = NX * NY * NC
 GROUP = NX * V
-BLOCK = NC * GROUP
-COLS = NR * V
-ROWS = NZ * V
+ROWS = NY * GROUP
+HALF = NZ * V
+COLS = NC * HALF
 TILE = 256
 ORDER = (0, 1, 7, 2, 6, 3, 5, 4)
 
@@ -53,9 +52,9 @@
 
 def kernel(
     proj_hbm, partner_hbm, losses_ref, grad_ref,
-    proj_ref, partner_ref, ur, cu, probs, acc, ut, uts, plain, tps, tp, to, tr, sbuf, rbuf,
+    proj_ref, partner_ref, ur, cu, cut, probs, acc, both, tps, tp, tr, sbuf, rbuf, kbuf, mbuf,
     in_sem, x_send, x_recv, y_send, y_recv, k_send, k_recv, z_send, z_recv,
-    tp_send, tp_recv, tr_send, tr_recv, tc_send, tc_recv, o_send, o_recv,
+    tp_send, tp_recv, tr_send, tr_recv, o_send, o_recv, m_send, m_recv,
 ):
     proj_copy = pltpu.make_async_copy(proj_hbm, proj_ref, in_sem.at[0])
     partner_copy = pltpu.make_async_copy(partner_hbm, partner_ref, in_sem.at[1])
@@ -109,7 +108,7 @@
     pl.semaphore_wait(barrier, len(peers))
 
     def block(rank, dx):
-        return ur.at[pl.ds(rank * BLOCK + dx * V, V)]
+        return ur.at[pl.ds(rank * GROUP + dx * V, V)]
 
     def to_x(rank, dx):
         return remote(block(rank, 0), block(rank, dx), x_send.at[rank, dx], x_recv.at[rank, dx],
@@ -119,34 +118,30 @@
         for dx in (1, 3, 2):
             to_x(rank, dx).start()
 
-    def share(rank):
-        first = rank * BLOCK
-        return remote(ur.at[pl.ds(first, GROUP)], ur.at[pl.ds(first + GROUP, GROUP)],
-                      k_send.at[rank], k_recv.at[rank], device(0, 0, 0, 1))
-
-    def share_when_whole(rank):
+    def whole(rank):
         for dx in (1, 3, 2):
             to_x(rank, dx).wait_recv()
-        share(rank).start()
-
-    def scores(rank, k, diagonal=False):
-        first = pl.multiple_of((rank * NC + k) * GROUP, GROUP)
+
+    def turned(lane):
+        cut[:, pl.ds(lane, TILE)] = jnp.transpose(cu[pl.ds(lane, TILE), :])
+
+    def scores(rank, tiles, fresh=False):
+        first = pl.multiple_of(rank * GROUP, GROUP)
         rows = pl.ds(first, GROUP)
         units = ur[rows, :]
-        ut[:, rows] = jnp.transpose(units)
-        for lane in range(0, ROWS, TILE):
+        if 0 in tiles:
+            both[pl.ds(0, W), rows] = jnp.transpose(units)
+        for lane in tiles:
             lanes = pl.ds(lane, TILE)
-            dots = lax.dot_general(
-                units, cu[lanes, :], (((1,), (1,)), ((), ())), preferred_element_type=jnp.float32
-            )
+            dots = jnp.dot(units, cut[:, lanes], preferred_element_type=jnp.float32)
             values = jnp.exp2(dots * (inv_temp * log2e))
-            if diagonal and lane == 0:
+            if fresh and lane == 0:
                 left = lax.broadcasted_iota(jnp.int32, (GROUP, TILE), 0)
                 right = lax.broadcasted_iota(jnp.int32, (GROUP, TILE), 1)
                 values = jnp.where((left == right) & (left < V), 0.0, values)
             total = jnp.sum(values.reshape(GROUP // 8, 8, TILE), axis=0)
             probs[rows, lanes] = values.astype(jnp.bfloat16)
-            if diagonal:
+            if fresh:
                 acc[:, lanes] = total
             else:
                 acc[:, lanes] += total
@@ -163,36 +158,51 @@
         for rank in ranks:
             copies[rank - 1].wait_recv()
 
-    for rank in range(1, NY):
-        arrived(y_copies, rank)
-        pass_on(rank)
-    share_when_whole(0)
-    arrived(z_copies, *range(1, NZ))
-    scores(0, 0, True)
-
-    def own_core(rank, carry):
-        share_when_whole(rank)
-        scores(rank, 0)
+    def go_on(*ranks):
+        for rank in ranks:
+            arrived(y_copies, rank)
+            pass_on(rank)
+
+    go_on(1, 2)
+    arrived(z_copies, 1, 2)
+    turned(0)
+    whole(0)
+    scores(0, (0,), True)
+    go_on(3, 4)
+    arrived(z_copies, 3, 4, 5)
+    turned(TILE)
+    go_on(5, 6)
+    arrived(z_copies, 6, 7)
+    other = send(cu.at[pl.ds(0, HALF)], cu.at[pl.ds(HALF, HALF)], k_send, k_recv,
+                 device(0, 0, 0, 1))
+    go_on(7)
+    turned(2 * TILE)
+    scores(0, (TILE, 2 * TILE), True)
+    whole(1)
+    scores(1, range(0, HALF, TILE))
+    other.wait_recv()
+    for lane in range(HALF, COLS, TILE):
+        turned(lane)
+    scores(0, range(HALF, COLS, TILE), True)
+    scores(1, range(HALF, COLS, TILE))
+
+    def step(rank, carry):
+        whole(rank)
+        scores(rank, range(0, COLS, TILE))
         return carry
 
-    def other_core(rank, carry):
-        share(rank).wait_recv()
-        scores(rank, 1)
-        return carry
-
-    lax.fori_loop(1, NY, own_core, 0)
-    lax.fori_loop(0, NY, other_core, 0)
+    lax.fori_loop(2, NY, step, 0)
 
     sums = jnp.sum(acc[...], axis=0, keepdims=True)
-    for rank, part in enumerate(to_rows([sums[:, at:at + W] for at in range(0, ROWS, W)])):
+    for rank, part in enumerate(to_rows([sums[:, at:at + W] for at in range(0, COLS, W)])):
         tps[rank] = part
     p_totals = []
     for rank in range(NZ - 1, -1, -1):
-        if rank:
-            p_totals.append(send(tps, tp.at[rank], tp_send.at[rank], tp_recv.at[rank],
-                                 device(0, 0, ORDER[rank], 0)))
-        p_totals.append(send(tps.at[pl.ds(rank, 1)], to.at[pl.ds(rank, 1)], tc_send.at[rank],
-                             tc_recv.at[rank], device(0, 0, ORDER[rank], 1)))
+        for k in (0, 1):
+            if rank or k:
+                at = k * NZ + rank
+                p_totals.append(send(tps, tp.at[at], tp_send.at[at], tp_recv.at[at],
+                                     device(0, 0, ORDER[rank], k)))
 
     partner_copy.wait()
     pairs = lax.broadcasted_iota(jnp.int32, (V, V), 0) + (row * (NY * 2 * NC) + col) * V
@@ -204,24 +214,20 @@
         precision=lax.Precision.HIGHEST, preferred_element_type=jnp.float32,
     )[:1] * inv_temp
 
-    def plain_sums(*lanes):
-        for lane in lanes:
-            plain[:, pl.ds(lane, TILE)] = jnp.dot(
-                ut[...], probs[:, pl.ds(lane, TILE)], preferred_element_type=jnp.float32
-            )
-
-    plain_sums(0, TILE)
     for copy in p_totals:
         copy.wait_recv()
     where = {offset: rank for rank, offset in enumerate(ORDER)}
     totals_of = []
-    for rank in range(NZ):
-        total = tps[rank]
-        for sender in range(1, NZ):
-            total = total + tp[sender, where[(ORDER[rank] + ORDER[sender]) % NZ]]
-        totals_of.append(total)
+    totals_of = []
+    for k in range(NC):
+        for rank in range(NZ):
+            total = tps[k * NZ + rank]
+            for sender in range(1, NC * NZ):
+                there = where[(ORDER[rank] + ORDER[sender % NZ]) % NZ]
+                total = total + tp[sender, (k + sender // NZ) % NC * NZ + there]
+            totals_of.append(total)
     totals = totals_of[0]
-    tr[0] = jnp.concatenate([totals, jnp.sum(to[...], axis=0)], axis=0)
+    tr[0] = totals
     for rank in range(NY - 1, -1, -1):
         for dx in (2, 1, 3, 0):
             if rank or dx:
@@ -229,26 +235,36 @@
                        device(-dx, -ORDER[rank], 0, 0)).start()
     losses_ref[...] = jnp.log(totals[:, :V]) - positive
     inverse = [1.0 / part for part in to_lanes(totals_of)]
-    plain_sums(2 * TILE)
 
     rest = remote(tr.at[pl.ds(1, NX * NY - 1)], tr.at[pl.ds(1, NX * NY - 1)], tr_send, tr_recv,
                   (row, col))
     rest.wait_recv()
-    shares_of = tr[...].reshape(NY, NX, NC, W)
+    shares_of = tr[...].reshape(NY, NX, 1, W)
     scales = [1.0 / part for part in to_lanes([shares_of[:, dx] for dx in range(NX)])]
-    for at in range(0, COLS, W):
-        group, tile = at // GROUP, at % GROUP // W
-        factor = scales[tile][group // NC, group % NC:group % NC + 1]
-        uts[:, pl.ds(at, W)] = (ut[:, pl.ds(at, W)].astype(jnp.float32) * factor).astype(
-            jnp.bfloat16
-        )
+    for at in range(0, ROWS, W):
+        factor = scales[at % GROUP // W][at // GROUP]
+        both[pl.ds(W, W), pl.ds(at, W)] = (
+            both[pl.ds(0, W), pl.ds(at, W)].astype(jnp.float32) * factor
+        ).astype(jnp.bfloat16)
+
+    def parts(lane):
+        sums = jnp.dot(both[...], probs[:, pl.ds(lane, TILE)], preferred_element_type=jnp.float32)
+        factor = jnp.concatenate(inverse[lane // W:(lane + TILE) // W], axis=1)
+        return jnp.transpose(sums[:W] * factor + sums[W:])
+
+    added = {}
+    for lane in range(HALF - TILE, -1, -TILE):
+        at = pl.ds(lane, TILE)
+        kbuf[at, :] = parts(HALF + lane).astype(jnp.bfloat16)
+        added[lane] = send(kbuf.at[at], mbuf.at[at], m_send.at[lane // TILE],
+                           m_recv.at[lane // TILE], device(0, 0, 0, 1))
 
     outputs = []
-    for lane in range(ROWS - TILE, -1, -TILE):
+    for lane in range(HALF - TILE, -1, -TILE):
         lanes = pl.ds(lane, TILE)
-        sums = jnp.dot(uts[...], probs[:, lanes], preferred_element_type=jnp.float32)
-        factor = jnp.concatenate(inverse[lane // W:(lane + TILE) // W], axis=1)
-        part = jnp.transpose(plain[:, lanes] * factor + sums)
+        part = parts(lane)
+        added[lane].wait_recv()
+        part = part + mbuf[lanes, :].astype(jnp.float32)
         sbuf[lanes, :] = part.astype(jnp.bfloat16)
         for rank in range(NZ - 1, 0, -1):
             if lane <= rank * V < lane + TILE:
@@ -272,7 +288,6 @@
     for rank in range(NY):
         for dx in (1, 3, 2):
             to_x(rank, dx).wait_send()
-        share(rank).wait_send()
     rest.wait_send()
 
 
@@ -288,22 +303,22 @@
         scratch_shapes=[
             pltpu.VMEM((V, W), jnp.float32),
             pltpu.VMEM((1, V), jnp.int32),
+            pltpu.VMEM((ROWS, W), jnp.bfloat16),
             pltpu.VMEM((COLS, W), jnp.bfloat16),
-            pltpu.VMEM((ROWS, W), jnp.bfloat16),
-            pltpu.VMEM((COLS, ROWS), jnp.bfloat16),
-            pltpu.VMEM((8, ROWS), jnp.float32),
             pltpu.VMEM((W, COLS), jnp.bfloat16),
-            pltpu.VMEM((W, COLS), jnp.bfloat16),
-            pltpu.VMEM((W, ROWS), jnp.float32),
-            pltpu.VMEM((NZ, 1, W), jnp.float32),
-            pltpu.VMEM((NZ, NZ, 1, W), jnp.float32),
-            pltpu.VMEM((NZ, 1, W), jnp.float32),
-            pltpu.VMEM((NY * NX, NC, W), jnp.float32),
-            pltpu.VMEM((ROWS, W), jnp.bfloat16),
-            pltpu.VMEM((ROWS, W), jnp.bfloat16),
-            dma((2,)), dma((NY, NX)), dma((NY, NX)), dma((NY,)), dma((NY,)), dma((NY,)), dma((NY,)),
-            dma((NZ,)), dma((NZ,)), dma((NZ,)), dma((NZ,)), dma, dma, dma((NZ,)), dma((NZ,)),
-            dma((NZ,)), dma((NZ,)),
+            pltpu.VMEM((ROWS, COLS), jnp.bfloat16),
+            pltpu.VMEM((8, COLS), jnp.float32),
+            pltpu.VMEM((2 * W, ROWS), jnp.bfloat16),
+            pltpu.VMEM((NC * NZ, 1, W), jnp.float32),
+            pltpu.VMEM((NC * NZ, NC * NZ, 1, W), jnp.float32),
+            pltpu.VMEM((NX * NY, 1, W), jnp.float32),
+            pltpu.VMEM((HALF, W), jnp.bfloat16),
+            pltpu.VMEM((HALF, W), jnp.bfloat16),
+            pltpu.VMEM((HALF, W), jnp.bfloat16),
+            pltpu.VMEM((HALF, W), jnp.bfloat16),
+            dma((2,)), dma((NY, NX)), dma((NY, NX)), dma((NY,)), dma((NY,)), dma, dma,
+            dma((NZ,)), dma((NZ,)), dma((NC * NZ,)), dma((NC * NZ,)), dma, dma, dma((NZ,)), dma((NZ,)),
+            dma((HALF // TILE,)), dma((HALF // TILE,)),
         ],
         compiler_params=pltpu.CompilerParams(
             collective_id=0, has_side_effects=True, vmem_limit_bytes=48 * 1024 * 1024

time: 52.3 us -> 53.4 us (1.021)
  Pallas kernels: 50.4 us -> 51.5 us
    pallas_call x1, Pallas kernels: 50.4 us -> 51.5 us  [body(): pl.pallas_call(kernel, out_shape=(pltpu.VMEM((1, V), jnp.float32), pltpu....]
where the time goes in v4:
time: 53.4 us; the launch traced here: 53.3 us
  Pallas kernels  51.5 us (96%)
  local copies, waits for them, and re-layouts  1.13 us (2%)
  between operations  0.64 us (1%)
    pallas_call x1, Pallas kernels, body(): pl.pallas_call(kernel, out_shape=(pltpu.VMEM((1, V), jnp.float32), pltpu....  51.5 us
    unnamed x2, local copies, waits for them, and re-layouts  1.13 us

profile of v4, /device:TPU:1, one launch (start us, length us, event | category | flops | bytes accessed | tf_op | source)
XLA Modules:
  0.0 53.3 jit_solution(6284427968895772763)
XLA Ops:
  0.6 51.5 %shard_map.41 = (f32[1,96]{1,0:T(1,128)S(1)}, f32[96,128]{1,0:T(8,128)S(1)}) custom-call(f32[96,128]{1,0:T(8,128)} %proj_hbm.1, s32[1,96]{1,0:T(1,128)} %bitcast.3), custom_call_target="tpu_custom_call" | custom-call | tf_op jit(solution)/shard_map/pallas_call | solution.py:298
  52.1 0.5 copy.6
  52.6 0.6 %copy.7 = f32[96,128]{1,0:T(8,128)} copy(f32[96,128]{1,0:T(8,128)S(1)} %get-tuple-element.7) | data formatting | bytes 98304

commit v5 on v2

--- a/solution.py
+++ b/solution.py
@@ -94,7 +94,7 @@
     peers = [device(dx, 0, 0, 0) for dx in range(1, NX)]
     peers += [device(0, dy, 0, 0) for dy in range(1, NY)]
     peers += [device(0, 0, dz, 0) for dz in range(1, NZ)]
-    peers += [device(0, 0, dz, 1) for dz in range(NZ)]
+    peers += [device(0, 0, 0, 1)]
     for peer in peers:
         pl.semaphore_signal(barrier, inc=1, device_id=peer, device_id_type=MESH)
 
@@ -129,35 +129,43 @@
             to_x(rank, dx).wait_recv()
         share(rank).start()
 
-    def scores(rank, k, diagonal=False):
-        first = pl.multiple_of((rank * NC + k) * GROUP, GROUP)
-        rows = pl.ds(first, GROUP)
-        units = ur[rows, :]
-        ut[:, rows] = jnp.transpose(units)
+    def scores(rank, diagonal=False):
+        first = pl.multiple_of(rank * BLOCK, BLOCK)
+        ut[:, pl.ds(first, BLOCK)] = jnp.transpose(ur[pl.ds(first, BLOCK), :])
         for lane in range(0, ROWS, TILE):
             lanes = pl.ds(lane, TILE)
-            dots = lax.dot_general(
-                units, cu[lanes, :], (((1,), (1,)), ((), ())), preferred_element_type=jnp.float32
-            )
-            values = jnp.exp2(dots * (inv_temp * log2e))
-            if diagonal and lane == 0:
-                left = lax.broadcasted_iota(jnp.int32, (GROUP, TILE), 0)
-                right = lax.broadcasted_iota(jnp.int32, (GROUP, TILE), 1)
-                values = jnp.where((left == right) & (left < V), 0.0, values)
-            total = jnp.sum(values.reshape(GROUP // 8, 8, TILE), axis=0)
-            probs[rows, lanes] = values.astype(jnp.bfloat16)
+            others = cu[lanes, :]
+            total = None
+            for at in range(0, BLOCK, TILE):
+                rows = pl.ds(first + at, TILE)
+                dots = lax.dot_general(
+                    ur[rows, :], others, (((1,), (1,)), ((), ())),
+                    preferred_element_type=jnp.float32,
+                )
+                values = jnp.exp2(dots * (inv_temp * log2e))
+                if diagonal and lane == 0 and at == 0:
+                    left = lax.broadcasted_iota(jnp.int32, (TILE, TILE), 0)
+                    right = lax.broadcasted_iota(jnp.int32, (TILE, TILE), 1)
+                    values = jnp.where((left == right) & (left < V), 0.0, values)
+                sums = jnp.sum(values.reshape(TILE // 8, 8, TILE), axis=0)
+                total = sums if total is None else total + sums
+                probs[rows, lanes] = values.astype(jnp.bfloat16)
             if diagonal:
                 acc[:, lanes] = total
             else:
                 acc[:, lanes] += total
 
+    y_copies = [
+        send(block(0, 0), block(rank, 0), y_send.at[rank], y_recv.at[rank],
+             device(0, -ORDER[rank], 0, 0))
+        for rank in range(1, NY)
+    ]
     pass_on(0)
-    y_copies, z_copies = [], []
-    for rank in range(1, NY):
-        y_copies.append(send(block(0, 0), block(rank, 0), y_send.at[rank], y_recv.at[rank],
-                             device(0, -ORDER[rank], 0, 0)))
-        z_copies.append(send(cu.at[pl.ds(0, V)], cu.at[pl.ds(rank * V, V)], z_send.at[rank],
-                             z_recv.at[rank], device(0, 0, -ORDER[rank], 0)))
+    z_copies = [
+        send(cu.at[pl.ds(0, V)], cu.at[pl.ds(rank * V, V)], z_send.at[rank], z_recv.at[rank],
+             device(0, 0, -ORDER[rank], 0))
+        for rank in range(1, NZ)
+    ]
 
     def arrived(copies, *ranks):
         for rank in ranks:
@@ -167,21 +175,21 @@
         arrived(y_copies, rank)
         pass_on(rank)
     share_when_whole(0)
+    share_when_whole(1)
+    share(0).wait_recv()
     arrived(z_copies, *range(1, NZ))
-    scores(0, 0, True)
-
-    def own_core(rank, carry):
-        share_when_whole(rank)
-        scores(rank, 0)
+    scores(0, True)
+
+    def step(rank, carry):
+        @pl.when(rank < NY - 1)
+        def _():
+            share_when_whole(rank + 1)
+
+        share(rank).wait_recv()
+        scores(rank)
         return carry
 
-    def other_core(rank, carry):
-        share(rank).wait_recv()
-        scores(rank, 1)
-        return carry
-
-    lax.fori_loop(1, NY, own_core, 0)
-    lax.fori_loop(0, NY, other_core, 0)
+    lax.fori_loop(1, NY, step, 0)
 
     sums = jnp.sum(acc[...], axis=0, keepdims=True)
     for rank, part in enumerate(to_rows([sums[:, at:at + W] for at in range(0, ROWS, W)])):
@@ -211,16 +219,23 @@
             )
 
     plain_sums(0, TILE)
+    for copy in started:
+        copy.wait_send()
+    for rank in range(NY):
+        for dx in (1, 3, 2):
+            to_x(rank, dx).wait_send()
+        share(rank).wait_send()
     for copy in p_totals:
         copy.wait_recv()
     where = {offset: rank for rank, offset in enumerate(ORDER)}
-    totals_of = []
-    for rank in range(NZ):
+
+    def totals_for(rank):
         total = tps[rank]
         for sender in range(1, NZ):
             total = total + tp[sender, where[(ORDER[rank] + ORDER[sender]) % NZ]]
-        totals_of.append(total)
-    totals = totals_of[0]
+        return total
+
+    totals = totals_for(0)
     tr[0] = jnp.concatenate([totals, jnp.sum(to[...], axis=0)], axis=0)
     for rank in range(NY - 1, -1, -1):
         for dx in (2, 1, 3, 0):
@@ -228,7 +243,7 @@
                 remote(tr.at[pl.ds(0, 1)], tr.at[pl.ds(rank * NX + dx, 1)], tr_send, tr_recv,
                        device(-dx, -ORDER[rank], 0, 0)).start()
     losses_ref[...] = jnp.log(totals[:, :V]) - positive
-    inverse = [1.0 / part for part in to_lanes(totals_of)]
+    inverse = [1.0 / part for part in to_lanes([totals] + [totals_for(rank) for rank in range(1, NZ)])]
     plain_sums(2 * TILE)
 
     rest = remote(tr.at[pl.ds(1, NX * NY - 1)], tr.at[pl.ds(1, NX * NY - 1)], tr_send, tr_recv,
@@ -267,12 +282,8 @@
     inner = jnp.sum(proj * dunit, axis=1, keepdims=True)
     grad_ref[...] = scale * dunit - scale * scale * scale * proj * inner
 
-    for copy in started:
+    for _, copy in outputs:
         copy.wait_send()
-    for rank in range(NY):
-        for dx in (1, 3, 2):
-            to_x(rank, dx).wait_send()
-        share(rank).wait_send()
     rest.wait_send()
 
 

time: 52.3 us -> 51.3 us (0.981)
  Pallas kernels: 50.4 us -> 49.4 us
    pallas_call x1, Pallas kernels: 50.4 us -> 49.4 us  [body(): pl.pallas_call(kernel, out_shape=(pltpu.VMEM((1, V), jnp.float32), pltpu....]
where the time goes in v5:
time: 51.3 us; the launch traced here: 51.1 us
  Pallas kernels  49.4 us (96%)
  local copies, waits for them, and re-layouts  1.13 us (2%)
  between operations  0.64 us (1%)
    pallas_call x1, Pallas kernels, body(): pl.pallas_call(kernel, out_shape=(pltpu.VMEM((1, V), jnp.float32), pltpu....  49.4 us
    unnamed x2, local copies, waits for them, and re-layouts  1.13 us

profile of v5, /device:TPU:1, one launch (start us, length us, event | category | flops | bytes accessed | tf_op | source)
XLA Modules:
  0.0 51.1 jit_solution(11620015080311897862)
XLA Ops:
  0.6 49.4 %shard_map.41 = (f32[1,96]{1,0:T(1,128)S(1)}, f32[96,128]{1,0:T(8,128)S(1)}) custom-call(f32[96,128]{1,0:T(8,128)} %proj_hbm.1, s32[1,96]{1,0:T(1,128)} %bitcast.3), custom_call_target="tpu_custom_call" | custom-call | tf_op jit(solution)/shard_map/pallas_call | solution.py:294
  50.0 0.5 %copy.6 = f32[96]{0:T(128)} copy(f32[96]{0:T(128)S(1)} %bitcast.2) | data formatting | bytes 768
  50.5 0.6 %copy.7 = f32[96,128]{1,0:T(8,128)} copy(f32[96,128]{1,0:T(8,128)S(1)} %get-tuple-element.7) | data formatting | bytes 98304

commit v6 on v5

--- a/solution.py
+++ b/solution.py
@@ -53,7 +53,7 @@
 
 def kernel(
     proj_hbm, partner_hbm, losses_ref, grad_ref,
-    proj_ref, partner_ref, ur, cu, probs, acc, ut, uts, plain, tps, tp, to, tr, sbuf, rbuf,
+    proj_ref, partner_ref, ur, cu, probs, acc, both, invr, scale_of, own_part, tps, tp, to, tr, sbuf, rbuf,
     in_sem, x_send, x_recv, y_send, y_recv, k_send, k_recv, z_send, z_recv,
     tp_send, tp_recv, tr_send, tr_recv, tc_send, tc_recv, o_send, o_recv,
 ):
@@ -99,6 +99,7 @@
         pl.semaphore_signal(barrier, inc=1, device_id=peer, device_id_type=MESH)
 
     tps[...] = jnp.ones_like(tps)
+    acc[...] = jnp.zeros_like(acc)
     proj_copy.wait()
     proj = proj_ref[...]
     scale = lax.rsqrt(jnp.sum(proj * proj, axis=1, keepdims=True) + epsilon)
@@ -129,9 +130,10 @@
             to_x(rank, dx).wait_recv()
         share(rank).start()
 
-    def scores(rank, diagonal=False):
+    def scores(rank):
         first = pl.multiple_of(rank * BLOCK, BLOCK)
-        ut[:, pl.ds(first, BLOCK)] = jnp.transpose(ur[pl.ds(first, BLOCK), :])
+        last = jnp.where(rank == 0, V, 0)
+        both[pl.ds(0, W), pl.ds(first, BLOCK)] = jnp.transpose(ur[pl.ds(first, BLOCK), :])
         for lane in range(0, ROWS, TILE):
             lanes = pl.ds(lane, TILE)
             others = cu[lanes, :]
@@ -143,17 +145,14 @@
                     preferred_element_type=jnp.float32,
                 )
                 values = jnp.exp2(dots * (inv_temp * log2e))
-                if diagonal and lane == 0 and at == 0:
+                if lane == 0 and at == 0:
                     left = lax.broadcasted_iota(jnp.int32, (TILE, TILE), 0)
                     right = lax.broadcasted_iota(jnp.int32, (TILE, TILE), 1)
-                    values = jnp.where((left == right) & (left < V), 0.0, values)
+                    values = jnp.where((left == right) & (left < last), 0.0, values)
                 sums = jnp.sum(values.reshape(TILE // 8, 8, TILE), axis=0)
                 total = sums if total is None else total + sums
                 probs[rows, lanes] = values.astype(jnp.bfloat16)
-            if diagonal:
-                acc[:, lanes] = total
-            else:
-                acc[:, lanes] += total
+            acc[:, lanes] += total
 
     y_copies = [
         send(block(0, 0), block(rank, 0), y_send.at[rank], y_recv.at[rank],
@@ -175,10 +174,7 @@
         arrived(y_copies, rank)
         pass_on(rank)
     share_when_whole(0)
-    share_when_whole(1)
-    share(0).wait_recv()
     arrived(z_copies, *range(1, NZ))
-    scores(0, True)
 
     def step(rank, carry):
         @pl.when(rank < NY - 1)
@@ -189,7 +185,7 @@
         scores(rank)
         return carry
 
-    lax.fori_loop(1, NY, step, 0)
+    lax.fori_loop(0, NY, step, 0)
 
     sums = jnp.sum(acc[...], axis=0, keepdims=True)
     for rank, part in enumerate(to_rows([sums[:, at:at + W] for at in range(0, ROWS, W)])):
@@ -212,13 +208,6 @@
         precision=lax.Precision.HIGHEST, preferred_element_type=jnp.float32,
     )[:1] * inv_temp
 
-    def plain_sums(*lanes):
-        for lane in lanes:
-            plain[:, pl.ds(lane, TILE)] = jnp.dot(
-                ut[...], probs[:, pl.ds(lane, TILE)], preferred_element_type=jnp.float32
-            )
-
-    plain_sums(0, TILE)
     for copy in started:
         copy.wait_send()
     for rank in range(NY):
@@ -244,34 +233,52 @@
                        device(-dx, -ORDER[rank], 0, 0)).start()
     losses_ref[...] = jnp.log(totals[:, :V]) - positive
     inverse = [1.0 / part for part in to_lanes([totals] + [totals_for(rank) for rank in range(1, NZ)])]
-    plain_sums(2 * TILE)
+    for index, part in enumerate(inverse):
+        invr[:, pl.ds(index * W, W)] = part
 
     rest = remote(tr.at[pl.ds(1, NX * NY - 1)], tr.at[pl.ds(1, NX * NY - 1)], tr_send, tr_recv,
                   (row, col))
     rest.wait_recv()
     shares_of = tr[...].reshape(NY, NX, NC, W)
     scales = [1.0 / part for part in to_lanes([shares_of[:, dx] for dx in range(NX)])]
-    for at in range(0, COLS, W):
-        group, tile = at // GROUP, at % GROUP // W
-        factor = scales[tile][group // NC, group % NC:group % NC + 1]
-        uts[:, pl.ds(at, W)] = (ut[:, pl.ds(at, W)].astype(jnp.float32) * factor).astype(
-            jnp.bfloat16
-        )
-
-    outputs = []
-    for lane in range(ROWS - TILE, -1, -TILE):
-        lanes = pl.ds(lane, TILE)
-        sums = jnp.dot(uts[...], probs[:, lanes], preferred_element_type=jnp.float32)
-        factor = jnp.concatenate(inverse[lane // W:(lane + TILE) // W], axis=1)
-        part = jnp.transpose(plain[:, lanes] * factor + sums)
+    for tile, part in enumerate(scales):
+        scale_of[tile] = part
+
+    def scaled(rank, carry):
+        for k in range(NC):
+            for tile in range(GROUP // W):
+                at = pl.ds(pl.multiple_of(rank * BLOCK, BLOCK) + k * GROUP + tile * W, W)
+                factor = scale_of[tile, rank][k:k + 1]
+                both[pl.ds(W, W), at] = (
+                    both[pl.ds(0, W), at].astype(jnp.float32) * factor
+                ).astype(jnp.bfloat16)
+        return carry
+
+    lax.fori_loop(0, NY, scaled, 0)
+
+    outputs = [
+        (rank, remote(sbuf.at[pl.ds(rank * V, V)], rbuf.at[pl.ds(rank * V, V)], o_send.at[rank],
+                      o_recv.at[rank], device(0, 0, ORDER[rank], 0)))
+        for rank in range(NZ - 1, 0, -1)
+    ]
+    tiles = ROWS // TILE
+
+    def weighted(now, carry):
+        lanes = pl.ds(pl.multiple_of((tiles - 1 - now) * TILE, TILE), TILE)
+        sums = jnp.dot(both[...], probs[:, lanes], preferred_element_type=jnp.float32)
+        part = jnp.transpose(sums[:W] * invr[:, lanes] + sums[W:])
         sbuf[lanes, :] = part.astype(jnp.bfloat16)
-        for rank in range(NZ - 1, 0, -1):
-            if lane <= rank * V < lane + TILE:
-                at = pl.ds(rank * V, V)
-                copy = send(sbuf.at[at], rbuf.at[at], o_send.at[rank], o_recv.at[rank],
-                            device(0, 0, ORDER[rank], 0))
-                outputs.append((rank, copy))
-    kept = part[:V]
+        own_part[...] = part
+        for tile in range(tiles):
+            @pl.when(now == tiles - 1 - tile)
+            def _():
+                for rank, copy in outputs:
+                    if tile * TILE <= rank * V < (tile + 1) * TILE:
+                        copy.start()
+        return carry
+
+    lax.fori_loop(0, tiles, weighted, 0)
+    kept = own_part[pl.ds(0, V), :]
     result = kept - 2.0 * partner_unit
     for rank, copy in outputs:
         copy.wait_recv()
@@ -303,9 +310,10 @@
             pltpu.VMEM((ROWS, W), jnp.bfloat16),
             pltpu.VMEM((COLS, ROWS), jnp.bfloat16),
             pltpu.VMEM((8, ROWS), jnp.float32),
-            pltpu.VMEM((W, COLS), jnp.bfloat16),
-            pltpu.VMEM((W, COLS), jnp.bfloat16),
-            pltpu.VMEM((W, ROWS), jnp.float32),
+            pltpu.VMEM((2 * W, COLS), jnp.bfloat16),
+            pltpu.VMEM((1, ROWS), jnp.float32),
+            pltpu.VMEM((GROUP // W, NY, NC, W), jnp.float32),
+            pltpu.VMEM((TILE, W), jnp.float32),
             pltpu.VMEM((NZ, 1, W), jnp.float32),
             pltpu.VMEM((NZ, NZ, 1, W), jnp.float32),
             pltpu.VMEM((NZ, 1, W), jnp.float32),

time: 51.3 us -> 52.1 us (1.016)
  Pallas kernels: 49.4 us -> 50.1 us
    pallas_call x1, Pallas kernels: 49.4 us -> 50.1 us  [body(): pl.pallas_call(kernel, out_shape=(pltpu.VMEM((1, V), jnp.float32), pltpu....]
where the time goes in v6:
time: 52.1 us; the launch traced here: 51.9 us
  Pallas kernels  50.1 us (96%)
  local copies, waits for them, and re-layouts  1.13 us (2%)
  between operations  0.64 us (1%)
    pallas_call x1, Pallas kernels, body(): pl.pallas_call(kernel, out_shape=(pltpu.VMEM((1, V), jnp.float32), pltpu....  50.1 us
    unnamed x2, local copies, waits for them, and re-layouts  1.13 us

profile of v6, /device:TPU:1, one launch (start us, length us, event | category | flops | bytes accessed | tf_op | source)
XLA Modules:
  0.0 51.9 jit_solution(13657651753832093213)
XLA Ops:
  0.6 50.1 %shard_map.41 = (f32[1,96]{1,0:T(1,128)S(1)}, f32[96,128]{1,0:T(8,128)S(1)}) custom-call(f32[96,128]{1,0:T(8,128)} %proj_hbm.1, s32[1,96]{1,0:T(1,128)} %bitcast.3), custom_call_target="tpu_custom_call" | custom-call | tf_op jit(solution)/shard_map/pallas_call | solution.py:301
  50.8 0.5 copy.6
  51.3 0.6 %copy.7 = f32[96,128]{1,0:T(8,128)} copy(f32[96,128]{1,0:T(8,128)S(1)} %get-tuple-element.7) | data formatting | bytes 98304

commit v7 on v5

--- a/solution.py
+++ b/solution.py
@@ -53,7 +53,7 @@
 
 def kernel(
     proj_hbm, partner_hbm, losses_ref, grad_ref,
-    proj_ref, partner_ref, ur, cu, probs, acc, ut, uts, plain, tps, tp, to, tr, sbuf, rbuf,
+    proj_ref, partner_ref, ur, cu, cut, probs, acc, ut, uts, plain, tps, tp, to, tr, sbuf, rbuf,
     in_sem, x_send, x_recv, y_send, y_recv, k_send, k_recv, z_send, z_recv,
     tp_send, tp_recv, tr_send, tr_recv, tc_send, tc_recv, o_send, o_recv,
 ):
@@ -129,28 +129,27 @@
             to_x(rank, dx).wait_recv()
         share(rank).start()
 
-    def scores(rank, diagonal=False):
-        first = pl.multiple_of(rank * BLOCK, BLOCK)
-        ut[:, pl.ds(first, BLOCK)] = jnp.transpose(ur[pl.ds(first, BLOCK), :])
-        for lane in range(0, ROWS, TILE):
+    def turned(lane):
+        cut[:, pl.ds(lane, TILE)] = jnp.transpose(cu[pl.ds(lane, TILE), :])
+
+    def scores(rank, k, tiles=range(0, ROWS, TILE)):
+        first_group = isinstance(rank, int) and rank == 0 and k == 0
+        first = pl.multiple_of((rank * NC + k) * GROUP, GROUP)
+        rows = pl.ds(first, GROUP)
+        units = ur[rows, :]
+        if 0 in tiles:
+            ut[:, rows] = jnp.transpose(units)
+        for lane in tiles:
             lanes = pl.ds(lane, TILE)
-            others = cu[lanes, :]
-            total = None
-            for at in range(0, BLOCK, TILE):
-                rows = pl.ds(first + at, TILE)
-                dots = lax.dot_general(
-                    ur[rows, :], others, (((1,), (1,)), ((), ())),
-                    preferred_element_type=jnp.float32,
-                )
-                values = jnp.exp2(dots * (inv_temp * log2e))
-                if diagonal and lane == 0 and at == 0:
-                    left = lax.broadcasted_iota(jnp.int32, (TILE, TILE), 0)
-                    right = lax.broadcasted_iota(jnp.int32, (TILE, TILE), 1)
-                    values = jnp.where((left == right) & (left < V), 0.0, values)
-                sums = jnp.sum(values.reshape(TILE // 8, 8, TILE), axis=0)
-                total = sums if total is None else total + sums
-                probs[rows, lanes] = values.astype(jnp.bfloat16)
-            if diagonal:
+            dots = jnp.dot(units, cut[:, lanes], preferred_element_type=jnp.float32)
+            values = jnp.exp2(dots * (inv_temp * log2e))
+            if first_group and lane == 0:
+                left = lax.broadcasted_iota(jnp.int32, (GROUP, TILE), 0)
+                right = lax.broadcasted_iota(jnp.int32, (GROUP, TILE), 1)
+                values = jnp.where((left == right) & (left < V), 0.0, values)
+            total = jnp.sum(values.reshape(GROUP // 8, 8, TILE), axis=0)
+            probs[rows, lanes] = values.astype(jnp.bfloat16)
+            if first_group:
                 acc[:, lanes] = total
             else:
                 acc[:, lanes] += total
@@ -171,25 +170,47 @@
         for rank in ranks:
             copies[rank - 1].wait_recv()
 
-    for rank in range(1, NY):
-        arrived(y_copies, rank)
-        pass_on(rank)
+    def go_on(*ranks):
+        for rank in ranks:
+            arrived(y_copies, rank)
+            pass_on(rank)
+
+    go_on(1, 2)
     share_when_whole(0)
-    share_when_whole(1)
+    arrived(z_copies, 1, 2)
+    turned(0)
+    scores(0, 0, (0,))
+    go_on(3, 4)
+    arrived(z_copies, 3, 4, 5)
+    turned(TILE)
+    scores(0, 0, (TILE,))
+    go_on(5, 6)
     share(0).wait_recv()
-    arrived(z_copies, *range(1, NZ))
-    scores(0, True)
-
-    def step(rank, carry):
-        @pl.when(rank < NY - 1)
-        def _():
-            share_when_whole(rank + 1)
-
+    scores(0, 1, (0, TILE))
+    go_on(7)
+    arrived(z_copies, 6, 7)
+    turned(2 * TILE)
+    scores(0, 0, (2 * TILE,))
+    scores(0, 1, (2 * TILE,))
+
+    def own_core(rank, carry):
+        share_when_whole(rank)
+        scores(rank, 0)
+        return carry
+
+    def other_core(rank, carry):
         share(rank).wait_recv()
-        scores(rank)
+        scores(rank, 1)
         return carry
 
-    lax.fori_loop(1, NY, step, 0)
+    def both_cores(rank, carry):
+        own_core(rank, carry)
+        other_core(rank - 1, carry)
+        return carry
+
+    own_core(1, 0)
+    lax.fori_loop(2, NY, both_cores, 0)
+    other_core(NY - 1, 0)
 
     sums = jnp.sum(acc[...], axis=0, keepdims=True)
     for rank, part in enumerate(to_rows([sums[:, at:at + W] for at in range(0, ROWS, W)])):
@@ -301,6 +322,7 @@
             pltpu.VMEM((1, V), jnp.int32),
             pltpu.VMEM((COLS, W), jnp.bfloat16),
             pltpu.VMEM((ROWS, W), jnp.bfloat16),
+            pltpu.VMEM((W, ROWS), jnp.bfloat16),
             pltpu.VMEM((COLS, ROWS), jnp.bfloat16),
             pltpu.VMEM((8, ROWS), jnp.float32),
             pltpu.VMEM((W, COLS), jnp.bfloat16),

time: 51.3 us -> 51.2 us (level)
  no operation moved by 1% of the time
where the time goes in v7:
time: 51.2 us; the launch traced here: 51.1 us
  Pallas kernels  49.3 us (96%)
  local copies, waits for them, and re-layouts  1.13 us (2%)
  between operations  0.64 us (1%)
    pallas_call x1, Pallas kernels, body(): pl.pallas_call(kernel, out_shape=(pltpu.VMEM((1, V), jnp.float32), pltpu....  49.3 us
    unnamed x2, local copies, waits for them, and re-layouts  1.13 us

profile of v7, /device:TPU:1, one launch (start us, length us, event | category | flops | bytes accessed | tf_op | source)
XLA Modules:
  0.0 51.1 jit_solution(12449116419659630358)
XLA Ops:
  0.6 49.3 %shard_map.41 = (f32[1,96]{1,0:T(1,128)S(1)}, f32[96,128]{1,0:T(8,128)S(1)}) custom-call(f32[96,128]{1,0:T(8,128)} %proj_hbm.1, s32[1,96]{1,0:T(1,128)} %bitcast.3), custom_call_target="tpu_custom_call" | custom-call | tf_op jit(solution)/shard_map/pallas_call | solution.py:315
  49.9 0.5 %copy.6 = f32[96]{0:T(128)} copy(f32[96]{0:T(128)S(1)} %bitcast.2) | data formatting | bytes 768
  50.5 0.6 %copy.7 = f32[96,128]{1,0:T(8,128)} copy(f32[96,128]{1,0:T(8,128)S(1)} %get-tuple-element.7) | data formatting | bytes 98304
